TPU v7x, 256 devices: a whole 4x4x8 slice. The times are simulated.
256 devices in a mesh: mp: 32 (over z, y), tok: 8 (over x, core).
Axes of the slice: x: 4, y: 4, z: 8, core: 2. Of those that a mesh axis runs over, the one named last changes fastest.
Arguments:
- hidden: bfloat16 [2048, 32768], P('tok', 'mp'), may hold values from -6 to 6
- sign_bits: int32 [32768], P('mp'), may hold values from 0 to 1
- down_weight: int32 [32768, 16384], P('mp', 'tok'), may hold values from -127 to 127
- exponents: int32 [16384], P('tok'), may hold values from 12 to 14
- residual: bfloat16 [2048, 16384], P('mp', 'tok'), may hold values from -6 to 6
Outputs:
- updated: bfloat16 [2048, 16384], P('mp', 'tok')
All inputs are finite; a program needn't handle non-finite values.
Results may differ from a plain program's by a relative error of at most 0.0046.
Values may be sent and summed in bfloat16 or wider, within the bound.
A program may use at most 128 MiB of HBM per device.

v0:
```python
import math

import jax
import jax.numpy as jnp
from jax import lax
from jax.sharding import PartitionSpec as P


def from_partner(block, axis, distance):
    count = lax.axis_size(axis)
    route = []
    for low in range(count):
        high = low | 1 << distance
        if high != low and high < count:
            route += [(low, high), (high, low)]
    return lax.ppermute(block, axis, route)


def walsh_matrix(order):
    bit_total = order.bit_length() - 1
    left = lax.broadcasted_iota(jnp.int32, (order, order), 0)
    right = lax.broadcasted_iota(jnp.int32, (order, order), 1)
    parity = jnp.zeros((order, order), jnp.int32)
    for level in range(bit_total):
        parity = parity + left // 2**level % 2 * (right // 2**level % 2)
    return (1 - 2 * (parity % 2)).astype(jnp.float32)


def per_device(hidden, sign_bits, down_weight, exponents, residual):
    axis_count = lax.axis_size("mp")
    unit_count = hidden.shape[1]
    inv_root = 1.0 / math.sqrt(unit_count * axis_count)
    flipped = hidden * (2 * sign_bits - 1).astype(jnp.bfloat16)
    local_walsh = walsh_matrix(unit_count).astype(jnp.bfloat16)
    current = jnp.dot(flipped, local_walsh, preferred_element_type=jnp.float32)
    own_index = lax.axis_index("mp")
    for bit_index in range(axis_count.bit_length() - 1):
        partner = from_partner(current, "mp", bit_index)
        own_bit = own_index // 2**bit_index % 2
        current = jnp.where(own_bit == 0, current + partner, partner - current)
    rotated = (current * inv_root).astype(jnp.bfloat16)
    gathered = lax.all_gather(rotated, "tok", axis=0, tiled=True)
    weight_bf = down_weight.astype(jnp.bfloat16)
    scales = jnp.exp2(-exponents.astype(jnp.float32))
    summed = lax.psum_scatter(
        jnp.dot(gathered, weight_bf, preferred_element_type=jnp.float32) * scales,
        "mp",
        scatter_dimension=0,
        tiled=True,
    )
    return (residual.astype(jnp.float32) + summed).astype(jnp.bfloat16)


def solution(mesh):
    return jax.shard_map(
        per_device,
        mesh=mesh,
        in_specs=(P("tok", "mp"), P("mp"), P("mp", "tok"), P("tok"), P("mp", "tok")),
        out_specs=P("mp", "tok"),
        check_vma=False,
    )
```

profile of v0, /device:TPU:2, one launch (start us, length us, event | category | flops | bytes accessed | tf_op | source)
XLA Modules:
  0.0 494.1 jit_solution(10133830975255373570)
XLA Ops:
  6.5 0.0 all-gather.2.cloned.1.call-start
  6.7 0.7 iota_shift-right-logical_fusion.8
  7.4 8.5 %fusion.49 = f32[256,1024]{1,0:T(8,128)S(1)} fusion(s32[1024]{0:T(1024)S(1)} %get-tuple-element.5, s32[1024]{0:T(1024)S(1)} %get-tuple-element.23, s32[1024]{0:T(1024)S(1)} %get-tuple-element.6, s32[1024]{0:T(1024)S(1)} %get-tuple-element.24, s32[1024]{0:T(1024)S(1)} %get-tuple-element.7, s32[1024]{0:T(1024)S(1)} %get-tuple-element.25, ...), kind=kOutput, calls=%fused_computation.147 | convolution fusion | flops 811859968 | bytes 1657856 | tf_op jit(solution)/shard_map/dot_general | solution.py:35
  15.9 1.7 collective-permute-start
  17.5 23.3 %collective-permute-done = f32[256,1024]{1,0:T(8,128)S(1)} collective-permute-done((f32[256,1024]{1,0:T(8,128)S(1)}, f32[256,1024]{1,0:T(8,128)S(1)}, u32[]{:S(2)}, u32[]{:S(2)}) %collective-permute-start) | collective-permute-done | bytes 1048608 | tf_op jit(solution)/shard_map/ppermute | solution.py:16
  40.9 0.2 subtract_select_fusion.3
  41.0 3.3 collective-permute-start.1
  44.3 22.3 %collective-permute-done.1 = f32[256,1024]{1,0:T(8,128)S(1)} collective-permute-done((f32[256,1024]{1,0:T(8,128)S(1)}, f32[256,1024]{1,0:T(8,128)S(1)}, u32[]{:S(2)}, u32[]{:S(2)}) %collective-permute-start.1) | collective-permute-done | bytes 1048608 | tf_op jit(solution)/shard_map/ppermute | solution.py:16
  66.7 0.2 subtract_select_fusion.2
  66.9 2.0 collective-permute-start.2
  68.9 0.0 copy-start.1
  68.9 21.4 %collective-permute-done.2 = f32[256,1024]{1,0:T(8,128)S(1)} collective-permute-done((f32[256,1024]{1,0:T(8,128)S(1)}, f32[256,1024]{1,0:T(8,128)S(1)}, u32[]{:S(2)}, u32[]{:S(2)}) %collective-permute-start.2) | collective-permute-done | bytes 1048608 | tf_op jit(solution)/shard_map/ppermute | solution.py:16
  90.3 0.2 subtract_select_fusion.1
  90.5 3.4 collective-permute-start.3
  93.9 43.1 %collective-permute-done.3 = f32[256,1024]{1,0:T(8,128)S(1)} collective-permute-done((f32[256,1024]{1,0:T(8,128)S(1)}, f32[256,1024]{1,0:T(8,128)S(1)}, u32[]{:S(2)}, u32[]{:S(2)}) %collective-permute-start.3) | collective-permute-done | bytes 1048608 | tf_op jit(solution)/shard_map/ppermute | solution.py:16
  137.0 0.2 subtract_select_fusion
  137.3 6.2 %collective-permute-start.4 = (f32[256,1024]{1,0:T(8,128)S(1)}, f32[256,1024]{1,0:T(8,128)S(1)}, u32[]{:S(2)}, u32[]{:S(2)}) collective-permute-start(f32[256,1024]{1,0:T(8,128)S(1)} %subtract_select_fusion), channel_id=1, source_target_pairs={{0,128},{128,0},{8,136},{136,8},{16,144},{144,16},{24,152},{152,24... | collective-permute-start | bytes 3145736 | tf_op jit(solution)/shard_map/ppermute | solution.py:16
  143.5 45.7 %collective-permute-done.4 = f32[256,1024]{1,0:T(8,128)S(1)} collective-permute-done((f32[256,1024]{1,0:T(8,128)S(1)}, f32[256,1024]{1,0:T(8,128)S(1)}, u32[]{:S(2)}, u32[]{:S(2)}) %collective-permute-start.4) | collective-permute-done | bytes 1048608 | tf_op jit(solution)/shard_map/ppermute | solution.py:16
  189.3 1.0 multiply_convert_fusion
  190.3 0.0 all-gather.2.cloned.1.call-update
  190.3 0.2 reduce-scatter.2.cloned.1.call-start
  190.6 0.0 copy-done.1
  190.6 32.4 %all-gather.2.cloned.1.call-done = bf16[2048,1024]{1,0:T(8,128)(2,1)} async-done(((bf16[256,1024]{1,0:T(8,128)(2,1)}), bf16[2048,1024]{1,0:T(8,128)(2,1)}) %all-gather.2.cloned.1.call-update) | async-done | bytes 4194320 | tf_op jit(solution)/shard_map/all_gather | solution.py:42
  223.0 15.8 %convolution_multiply_fusion = f32[2048,2048]{1,0:T(8,128)} fusion(bf16[2048,1024]{1,0:T(8,128)(2,1)} %all-gather.2.cloned.1.call-done, f32[2048]{0:T(1024)S(1)} %multiply_exponential_fusion, s32[1024,2048]{1,0:T(8,128)} %param.7), kind=kOutput, calls=%fused_computation | convolution fusion | flops 8596226048 | bytes 29368320 | tf_op jit(solution)/shard_map/dot_general | solution.py:46
  238.8 0.0 copy-start
  238.8 0.0 reduce-scatter.2.cloned.1.call-update
  238.8 246.6 %reduce-scatter.2.cloned.1.call-done = f32[64,2048]{1,0:T(8,128)} async-done(((f32[2048,2048]{1,0:T(8,128)}), f32[64,2048]{1,0:T(8,128)}) %reduce-scatter.2.cloned.1.call-update) | async-done | bytes 524304 | tf_op jit(solution)/shard_map/reduce_scatter | solution.py:45
  485.4 0.0 copy-done
  485.4 1.8 add_convert_fusion
  (15 shorter events, 0.1 us)
Async XLA Ops:
  6.5 216.5 %all-gather.2.cloned.1.call-start = ((), (), s32[]{:S(2)}) async-start(), calls=%async_computation.1 | async-start | bytes 4718592 | tf_op jit(solution)/shard_map/all_gather | solution.py:42
  15.9 25.0 %collective-permute-start = (f32[256,1024]{1,0:T(8,128)S(1)}, f32[256,1024]{1,0:T(8,128)S(1)}, u32[]{:S(2)}, u32[]{:S(2)}) collective-permute-start(f32[256,1024]{1,0:T(8,128)S(1)} %fusion.49), channel_id=1, source_target_pairs={{0,8},{8,0},{16,24},{24,16},{32,40},{40,32},{48,56},{56,48},{64,72... | collective-permute-start | bytes 3145736 | tf_op jit(solution)/shard_map/ppermute | solution.py:16
  41.0 25.6 %collective-permute-start.1 = (f32[256,1024]{1,0:T(8,128)S(1)}, f32[256,1024]{1,0:T(8,128)S(1)}, u32[]{:S(2)}, u32[]{:S(2)}) collective-permute-start(f32[256,1024]{1,0:T(8,128)S(1)} %subtract_select_fusion.3), channel_id=1, source_target_pairs={{0,16},{16,0},{8,24},{24,8},{32,48},{48,32},{40,56},{56,40},{64,80... | collective-permute-start | bytes 3145736 | tf_op jit(solution)/shard_map/ppermute | solution.py:16
  66.9 23.4 %collective-permute-start.2 = (f32[256,1024]{1,0:T(8,128)S(1)}, f32[256,1024]{1,0:T(8,128)S(1)}, u32[]{:S(2)}, u32[]{:S(2)}) collective-permute-start(f32[256,1024]{1,0:T(8,128)S(1)} %subtract_select_fusion.2), channel_id=1, source_target_pairs={{0,32},{32,0},{8,40},{40,8},{16,48},{48,16},{24,56},{56,24},{64,96... | collective-permute-start | bytes 3145736 | tf_op jit(solution)/shard_map/ppermute | solution.py:16
  68.9 121.7 %copy-start.1 = (s32[2048]{0:T(1024)S(1)}, s32[2048]{0:T(1024)}, u32[]{:S(2)}) copy-start(s32[2048]{0:T(1024)} %param.8) | copy-start | bytes 24580
  90.5 46.5 %collective-permute-start.3 = (f32[256,1024]{1,0:T(8,128)S(1)}, f32[256,1024]{1,0:T(8,128)S(1)}, u32[]{:S(2)}, u32[]{:S(2)}) collective-permute-start(f32[256,1024]{1,0:T(8,128)S(1)} %subtract_select_fusion.1), channel_id=1, source_target_pairs={{0,64},{64,0},{8,72},{72,8},{16,80},{80,16},{24,88},{88,24},{32,96... | collective-permute-start | bytes 3145736 | tf_op jit(solution)/shard_map/ppermute | solution.py:16
  137.3 52.0 %collective-permute-start.4 = (f32[256,1024]{1,0:T(8,128)S(1)}, f32[256,1024]{1,0:T(8,128)S(1)}, u32[]{:S(2)}, u32[]{:S(2)}) collective-permute-start(f32[256,1024]{1,0:T(8,128)S(1)} %subtract_select_fusion), channel_id=1, source_target_pairs={{0,128},{128,0},{8,136},{136,8},{16,144},{144,16},{24,152},{152,24... | collective-permute-start | bytes 3145736 | tf_op jit(solution)/shard_map/ppermute | solution.py:16
  190.3 295.1 %reduce-scatter.2.cloned.1.call-start = ((), (), s32[]{:S(2)}) async-start(), calls=%async_computation.2 | async-start | bytes 17301504 | tf_op jit(solution)/shard_map/reduce_scatter | solution.py:45
  238.8 246.7 %copy-start = (bf16[64,2048]{1,0:T(8,128)(2,1)S(1)}, bf16[64,2048]{1,0:T(8,128)(2,1)}, u32[]{:S(2)}) copy-start(bf16[64,2048]{1,0:T(8,128)(2,1)} %param.9) | copy-start | bytes 786436
Sparse Core Ops, SparseCore 0:
  190.4 32.4 all-gather.1
  238.9 246.4 reduce-scatter.1
where the time goes:
time: 494 us
  waiting for transfers between devices  435 us (88%)
  matrix products  24.2 us (5%)
  starting transfers between devices  16.8 us (3%)
  between operations  13.5 us (3%)
    reduce_scatter x1, waiting for transfers between devices, per_device(): lax.psum_scatter(jnp.dot(gathered, weight_bf, preferred_element_type=jnp....  247 us
    ppermute x5, waiting for transfers between devices, from_partner(): return lax.ppermute(block, axis, route)  156 us
    all_gather x1, waiting for transfers between devices, per_device(): gathered = lax.all_gather(rotated, 'tok', axis=0, tiled=True)  32.4 us
    ppermute x5, starting transfers between devices, from_partner(): return lax.ppermute(block, axis, route)  16.5 us
    dot_general x1, matrix products, per_device(): jnp.dot(gathered, weight_bf, preferred_element_type=jnp.float32) * scales  15.8 us
  transfers between devices with their start and end apart: 7, of which 7 were waited for; matrix products, arithmetic and copies ran while one was open for 0% of the time, Pallas kernels for 0%

commit v1 on v0

v1 whole, which is shorter than its diff:
```python
import functools
import math

import jax
import jax.numpy as jnp
from jax import lax
from jax.experimental import pallas as pl
from jax.experimental.pallas import tpu as pltpu
from jax.sharding import PartitionSpec as P

MESH = pl.DeviceIdType.MESH
F32, BF16 = jnp.float32, jnp.bfloat16
NZ, NY, NX = 8, 4, 4
NMP = NZ * NY
UNITS = 1024
LANES = 128
COLS = 2048
YW = 1280
ZW = COLS - YW
YH, ZH = YW // 2, ZW // 2
ROWS = 64


def butterfly(v):
    count = v.shape[0]
    rest = v.shape[1:]
    span = 1
    while span < count:
        pairs = v.reshape((count // (2 * span), 2, span) + rest)
        low, high = pairs[:, 0], pairs[:, 1]
        v = jnp.stack([low + high, low - high], axis=1).reshape((count,) + rest)
        span *= 2
    return v


def walsh(order):
    both = lax.broadcasted_iota(jnp.int32, (order, order), 0) & lax.broadcasted_iota(
        jnp.int32, (order, order), 1
    )
    both = both ^ (both >> 4)
    both = both ^ (both >> 2)
    both = both ^ (both >> 1)
    return (1 - 2 * (both & 1)).astype(F32).astype(BF16)


def send(src, dst, send_sem, recv_sem, device):
    pltpu.make_async_remote_copy(
        src_ref=src,
        dst_ref=dst,
        send_sem=send_sem,
        recv_sem=recv_sem,
        device_id=device,
        device_id_type=MESH,
    ).start()


def drain(buf, sem):
    pltpu.make_async_copy(buf, buf, sem).wait()


def kernel(
    hid, sgn, w_hbm, expo, res, out,
    slab, recv1, mid, rot, recv2, act, w, w32, part,
    ys1, yr1, ys2, yr2, zs1, zr1, zs2, zr2, us1, ur1, us2, ur2, vs1, vr1, vs2, vr2,
    w_sem, a1_sem, a2_send, a2_recv, ag_send, ag_direct, ag_core,
    y_send, yr1_sem, yr2_sem, z_send, zr1_sem, zr2_sem,
    u_send, ur1_sem, ur2_sem, v_send, vr1_sem, vr2_sem,
):
    m, t = lax.axis_index("mp"), lax.axis_index("tok")
    z, y = lax.div(m, NY), lax.rem(m, NY)
    x, core = lax.div(t, 2), lax.rem(t, 2)

    def zmod(v):
        return lax.rem(v + NZ, NZ)

    def ymod(v):
        return lax.rem(v + NY, NY)

    def at_zy(zz, yy):
        return (zz * NY + yy, t)

    def at_x(xx, cc):
        return (m, xx * 2 + cc)

    sibling = at_x(x, 1 - core)
    y_next = (at_zy(z, ymod(y + 1)), at_zy(z, ymod(y - 1)))
    z_next = (at_zy(zmod(z + 1), y), at_zy(zmod(z - 1), y))

    barrier = pltpu.get_barrier_semaphore()

    def greet(i, _):
        pl.semaphore_signal(
            barrier, inc=1, device_id=(lax.rem(m + i, NMP), t), device_id_type=MESH
        )
        return 0

    lax.fori_loop(1, NMP, greet, 0)
    for dx in (1, 2, 3):
        pl.semaphore_signal(
            barrier, inc=1, device_id=at_x(lax.rem(x + dx, NX), core), device_id_type=MESH
        )
    pl.semaphore_signal(barrier, inc=1, device_id=sibling, device_id_type=MESH)

    w_rows = UNITS // 8
    for i in range(8):
        rows = pl.ds(i * w_rows, w_rows)
        pltpu.make_async_copy(w_hbm.at[rows], w32.at[rows], w_sem.at[i]).start()

    signs = (2 * sgn[...] - 1).astype(F32)

    def build(j, _):
        rows = hid[pl.ds(pl.multiple_of(j * 16, 16), 16), :].astype(F32) * signs
        for half in range(2):
            group = 2 * j + half
            dest = lax.rem(group, NZ) * NY + lax.div(group, NZ)
            own = rows[half * 8:half * 8 + 8]
            tall = jnp.concatenate(
                [own[:, k * LANES:(k + 1) * LANES] for k in range(8)], axis=0
            )
            slab[dest] = tall.astype(BF16)
        return 0

    lax.fori_loop(0, 16, build, 0)
    pl.semaphore_wait(barrier, NMP - 1 + 4)

    def spread(i, _):
        dest = lax.rem(m + i, NMP)
        send(slab.at[dest], recv1.at[m], a1_sem.at[0], a1_sem.at[1], (dest, t))
        return 0

    lax.fori_loop(1, NMP, spread, 0)
    recv1[m] = slab[m]

    def convert(j, _):
        rows = pl.ds(pl.multiple_of(j * 16, 16), 16)
        w[rows, :] = w32[rows, :].astype(F32).astype(BF16)
        return 0

    for i in range(8):
        rows = pl.ds(i * w_rows, w_rows)
        pltpu.make_async_copy(w_hbm.at[rows], w32.at[rows], w_sem.at[i]).wait()
        lax.fori_loop(i * w_rows // 16, (i + 1) * w_rows // 16, convert, 0)
    small_walsh = walsh(LANES)

    drain(recv1.at[pl.ds(0, NMP - 1)], a1_sem.at[1])

    def rotate_low(i, _):
        blocks = pl.ds(i * 4, 4)
        lanes = jnp.dot(
            recv1[blocks].reshape(256, LANES), small_walsh, preferred_element_type=F32
        ).reshape(4, 8, 8, LANES)
        for b in range(4):
            mid[i * 4 + b] = butterfly(lanes[b]).reshape(ROWS, LANES)
        return 0

    lax.fori_loop(0, 8, rotate_low, 0)
    inv_root = 1.0 / math.sqrt(NMP * UNITS)

    def rotate_high(i, _):
        rows = pl.ds(pl.multiple_of(i * 16, 16), 16)
        rot[:, rows, :] = (butterfly(mid[:, rows, :]) * inv_root).astype(BF16)
        return 0

    lax.fori_loop(0, 4, rotate_high, 0)

    def give_back(j, to_y, first):
        def one(i, _):
            to_z = lax.rem(z + i, NZ)
            dest = to_z * NY + to_y
            send(rot.at[dest], recv2.at[j, z], a2_send, a2_recv.at[j], (dest, t))
            return 0

        lax.fori_loop(first, NZ, one, 0)

    give_back(0, ymod(y + 2), 0)
    give_back(1, ymod(y - 1), 0)
    give_back(2, ymod(y + 1), 0)
    give_back(3, y, 1)
    recv2[3, z] = rot[m]

    def gather_own(j):
        count = NZ if j < 3 else NZ - 1
        drain(recv2.at[j, pl.ds(0, count)], a2_recv.at[j])

        def one(i, _):
            pieces = []
            for half in range(2):
                tall = recv2[j, 2 * i + half].astype(F32)
                pieces.append(
                    jnp.concatenate([tall[k * 8:k * 8 + 8] for k in range(8)], axis=1)
                )
            rows = pl.ds(pl.multiple_of(i * 16, 16), 16)
            act[j, t, rows, :] = jnp.concatenate(pieces, axis=0).astype(BF16)
            return 0

        lax.fori_loop(0, 4, one, 0)
        mine = act.at[j, t]
        for i, dx in enumerate((1, 3, 2)):
            send(mine, mine, ag_send.at[j], ag_direct.at[j, i], at_x(lax.rem(x + dx, NX), core))
        send(mine, mine, ag_send.at[j], ag_core.at[j], sibling)

    def pass_on(j):
        for i, dx in enumerate((1, 3, 2)):
            piece = act.at[j, lax.rem(x - dx + NX, NX) * 2 + core]
            drain(piece, ag_direct.at[j, i])
            send(piece, piece, ag_send.at[j], ag_core.at[j], sibling)

    def multiply(j):
        drain(act.at[j, pl.ds(0, 4)], ag_core.at[j])

        def one(i, _):
            cols = pl.ds(pl.multiple_of(i * 256, 256), 256)
            part[j, :, :, cols] = jnp.dot(
                act[j].reshape(NZ * ROWS, UNITS), w[:, cols], preferred_element_type=F32
            ).reshape(NZ, ROWS, 256)
            return 0

        lax.fori_loop(0, COLS // 256, one, 0)

    def compose(d, step, j, zz, low, half, incoming, dst):
        this, other = d * half, (1 - d) * half
        if step == 1:
            dst[...] = part[j, zz, :, pl.ds(low + this, half)].astype(BF16)
        elif step == 2:
            dst[:, pl.ds(this, half)] = (
                part[j, zz, :, pl.ds(low + this, half)] + incoming[...].astype(F32)
            ).astype(BF16)
            dst[:, pl.ds(other, half)] = part[j, zz, :, pl.ds(low + other, half)].astype(BF16)
        else:
            dst[...] = (
                part[j, zz, :, pl.ds(low, 2 * half)] + incoming[...].astype(F32)
            ).astype(BF16)

    def z_target(d, step):
        return zmod(z + (5 - step) * (1 - 2 * d))

    def z_hop(j, step, low, half, s1, r1, s2, r2, s_sem, r1_sem, r2_sem):
        for d in range(2):
            zz = z_target(d, step)
            if step == 1:
                compose(d, 1, j, zz, low, half, None, s1.at[d])
                send(s1.at[d], r1.at[d], s_sem.at[0], r1_sem.at[d], z_next[d])
                continue
            if step == 2:
                incoming, sem = r1.at[d], r1_sem.at[d]
            else:
                incoming, sem = r2.at[d, step - 3], r2_sem.at[d, step - 3]
            drain(incoming, sem)
            compose(d, step, j, zz, low, half, incoming, s2.at[d, step - 2])
            send(
                s2.at[d, step - 2], r2.at[d, step - 2],
                s_sem.at[1], r2_sem.at[d, step - 2], z_next[d],
            )

    def z_first(j, step):
        z_hop(
            j, step, YW, ZH, zs1.at[j], zr1.at[j], zs2.at[j], zr2.at[j],
            z_send, zr1_sem.at[j], zr2_sem.at[j],
        )

    def z_first_end(j):
        for d in range(2):
            drain(zr2.at[j, d, 2], zr2_sem.at[j, d, 2])
        part[j, z, :, pl.ds(YW, ZW)] = (
            part[j, z, :, pl.ds(YW, ZW)] + zr2[j, 0, 2].astype(F32) + zr2[j, 1, 2].astype(F32)
        )

    def z_second(step):
        z_hop(3, step, 0, YH, us1, ur1, us2, ur2, u_send, ur1_sem, ur2_sem)

    def block_at(k):
        up = lax.div(k + 1, 2)
        return zmod(z + 4 + up * (1 - 2 * lax.rem(k + 1, 2)))

    def y_first_start(k, _):
        zz = block_at(k)
        for d in range(2):
            compose(d, 1, 0, zz, 0, YH, None, ys1.at[d, k])
            send(ys1.at[d, k], yr1.at[d, k], y_send.at[0], yr1_sem.at[d, k], y_next[d])
        return 0

    def y_first_pass(d):
        def one(k, _):
            zz = block_at(k)
            drain(yr1.at[d, k], yr1_sem.at[d, k])
            compose(d, 2, 1 + d, zz, 0, YH, yr1.at[d, k], ys2.at[d, k])
            send(ys2.at[d, k], yr2.at[d, k], y_send.at[1], yr2_sem.at[d, k], y_next[d])
            return 0

        return one

    def y_first_both(k, _):
        y_first_pass(0)(k, 0)
        y_first_pass(1)(k, 0)
        return 0

    def y_first_end(k, _):
        zz = block_at(k)
        for d in range(2):
            drain(yr2.at[d, k], yr2_sem.at[d, k])
        part[3, zz, :, pl.ds(0, YW)] = (
            part[3, zz, :, pl.ds(0, YW)] + yr2[0, k].astype(F32) + yr2[1, k].astype(F32)
        )
        return 0

    def y_second_start():
        for d in range(2):
            compose(d, 1, 0, z, YW, ZH, None, vs1.at[d])
            send(vs1.at[d], vr1.at[d], v_send.at[0], vr1_sem.at[d], y_next[d])

    def y_second_pass(d):
        drain(vr1.at[d], vr1_sem.at[d])
        compose(d, 2, 1 + d, z, YW, ZH, vr1.at[d], vs2.at[d])
        send(vs2.at[d], vr2.at[d], v_send.at[1], vr2_sem.at[d], y_next[d])

    gather_own(0)
    gather_own(1)
    pass_on(0)
    gather_own(2)
    gather_own(3)
    multiply(0)
    z_first(0, 1)
    lax.fori_loop(0, 8, y_first_start, 0)
    pass_on(1)
    multiply(1)
    z_first(1, 1)
    z_first(0, 2)
    lax.fori_loop(0, 2, y_first_pass(0), 0)
    pass_on(2)
    multiply(2)
    z_first(2, 1)
    z_first(1, 2)
    z_first(0, 3)
    lax.fori_loop(0, 2, y_first_pass(1), 0)
    lax.fori_loop(2, 4, y_first_both, 0)
    pass_on(3)
    multiply(3)
    z_first(3, 1)
    z_first(2, 2)
    z_first(1, 3)
    z_first(0, 4)
    lax.fori_loop(4, 8, y_first_both, 0)
    z_first(3, 2)
    z_first(2, 3)
    z_first(1, 4)
    z_first_end(0)
    y_second_start()
    lax.fori_loop(0, 1, y_first_end, 0)
    z_second(1)
    z_first(3, 3)
    z_first(2, 4)
    z_first_end(1)
    y_second_pass(0)
    lax.fori_loop(1, 3, y_first_end, 0)
    z_second(2)
    z_first(3, 4)
    z_first_end(2)
    y_second_pass(1)
    lax.fori_loop(3, 5, y_first_end, 0)
    z_second(3)
    z_first_end(3)
    lax.fori_loop(5, 7, y_first_end, 0)
    z_second(4)
    lax.fori_loop(7, 8, y_first_end, 0)

    scales = jnp.exp2(-expo[...].astype(F32))
    for d in range(2):
        drain(vr2.at[d], vr2_sem.at[d])
    total = part[3, z, :, pl.ds(YW, ZW)] + vr2[0].astype(F32) + vr2[1].astype(F32)
    out[:, YW:] = (res[:, YW:].astype(F32) + total * scales[:, YW:]).astype(BF16)
    for d in range(2):
        drain(ur2.at[d, 2], ur2_sem.at[d, 2])
    total = part[3, z, :, pl.ds(0, YW)] + ur2[0, 2].astype(F32) + ur2[1, 2].astype(F32)
    out[:, :YW] = (res[:, :YW].astype(F32) + total * scales[:, :YW]).astype(BF16)

    drain(slab.at[pl.ds(0, NMP - 1)], a1_sem.at[0])
    drain(rot.at[pl.ds(0, NMP - 1)], a2_send)
    for j in range(4):
        drain(act.at[j, pl.ds(0, 7)], ag_send.at[j])
    for buf, sem in (
        (ys1, y_send.at[0]), (ys2, y_send.at[1]), (zs1, z_send.at[0]), (zs2, z_send.at[1]),
        (us1, u_send.at[0]), (us2, u_send.at[1]), (vs1, v_send.at[0]), (vs2, v_send.at[1]),
    ):
        drain(buf, sem)


def per_device(hidden, sign_bits, down_weight, exponents, residual):
    vmem = pl.BlockSpec(memory_space=pltpu.VMEM)

    def pair(*shape):
        return [pltpu.VMEM(shape, BF16)] * 2

    dma = pltpu.SemaphoreType.DMA
    return pl.pallas_call(
        kernel,
        out_shape=jax.ShapeDtypeStruct((ROWS, COLS), BF16),
        in_specs=[vmem, vmem, pl.BlockSpec(memory_space=pl.ANY), vmem, vmem],
        out_specs=vmem,
        scratch_shapes=[
            pltpu.VMEM((NMP, ROWS, LANES), BF16),
            pltpu.VMEM((NMP, ROWS, LANES), BF16),
            pltpu.VMEM((NMP, ROWS, LANES), F32),
            pltpu.VMEM((NMP, ROWS, LANES), BF16),
            pltpu.VMEM((4, NZ, ROWS, LANES), BF16),
            pltpu.VMEM((4, NZ, ROWS, UNITS), BF16),
            pltpu.VMEM((UNITS, COLS), BF16),
            pltpu.VMEM((UNITS, COLS), jnp.int32),
            pltpu.VMEM((4, NZ, ROWS, COLS), F32),
            *pair(2, 8, ROWS, YH),
            *pair(2, 8, ROWS, YW),
            *pair(4, 2, ROWS, ZH),
            *pair(4, 2, 3, ROWS, ZW),
            *pair(2, ROWS, YH),
            *pair(2, 3, ROWS, YW),
            *pair(2, ROWS, ZH),
            *pair(2, ROWS, ZW),
            dma((8,)), dma((2,)), dma, dma((4,)), dma((4,)), dma((4, 3)), dma((4,)),
            dma((2,)), dma((2, 8)), dma((2, 8)), dma((2,)), dma((4, 2)), dma((4, 2, 3)),
            dma((2,)), dma((2,)), dma((2, 3)), dma((2,)), dma((2,)), dma((2,)),
        ],
        compiler_params=pltpu.CompilerParams(
            collective_id=0, has_side_effects=True, vmem_limit_bytes=60 * 2**20
        ),
        cost_estimate=pl.CostEstimate(
            flops=2 * 2048 * UNITS * COLS, bytes_accessed=10 * 2**20, transcendentals=0
        ),
    )(
        hidden,
        sign_bits.reshape(1, UNITS),
        down_weight,
        exponents.reshape(1, COLS),
        residual,
    )


def solution(mesh):
    return jax.shard_map(
        per_device,
        mesh=mesh,
        in_specs=(P("tok", "mp"), P("mp"), P("mp", "tok"), P("tok"), P("mp", "tok")),
        out_specs=P("mp", "tok"),
        check_vma=False,
    )
```

time: 494 us -> 116 us (0.23)
  waiting for transfers between devices: 435 us -> 0 us
  Pallas kernels: 0 us -> 113 us
  matrix products: 24.2 us -> 0 us
  starting transfers between devices: 16.8 us -> 0 us
  between operations: 13.5 us -> 0.01 us
    reduce_scatter x1 -> x0, waiting for transfers between devices: 247 us -> none  [per_device(): lax.psum_scatter(jnp.dot(gathered, weight_bf, preferred_element_type=jnp....]
    ppermute x5 -> x0, waiting for transfers between devices: 156 us -> none  [from_partner(): return lax.ppermute(block, axis, route)]
    pallas_call x0 -> x1, Pallas kernels: none -> 113 us  [per_device(): pl.pallas_call(kernel, out_shape=jax.ShapeDtypeStruct((ROWS, COLS), BF16)...]
    all_gather x1 -> x0, waiting for transfers between devices: 32.4 us -> none  [per_device(): gathered = lax.all_gather(rotated, 'tok', axis=0, tiled=True)]
    dot_general x2 -> x0, matrix products: 24.2 us -> none  [the longest x1 15.8 us: per_device(): jnp.dot(gathered, weight_bf, preferred_element_type=jnp.float32) * scales]
    ppermute x5 -> x0, starting transfers between devices: 16.5 us -> none  [from_partner(): return lax.ppermute(block, axis, route)]
  transfers between devices with their start and end apart: 7 -> 0, of which waited for: 7 -> 0; matrix products, arithmetic and copies ran while one was open for 0% -> 0% of each run, Pallas kernels for 0% -> 0%
where the time goes in v1:
time: 116 us; the launch traced here: 115 us
  Pallas kernels  113 us (97%)
  local copies, waits for them, and re-layouts  1.67 us (1%)
    pallas_call x1, Pallas kernels, per_device(): pl.pallas_call(kernel, out_shape=jax.ShapeDtypeStruct((ROWS, COLS), BF16)...  113 us

profile of v1, /device:TPU:2, one launch (start us, length us, event | category | flops | bytes accessed | tf_op | source)
XLA Modules:
  0.0 114.8 jit_solution(4195251748339652146)
XLA Ops:
  0.0 113.1 %shard_map.55 = bf16[64,2048]{1,0:T(8,128)(2,1)} custom-call(bf16[256,1024]{1,0:T(8,128)(2,1)} %hid.1, s32[1,1024]{1,0:T(1,128)} %bitcast.3, s32[1024,2048]{1,0:T(8,128)} %w_hbm.1, s32[1,2048]{1,0:T(1,128)} %bitcast.2, bf16[64,2048]{1,0:T(8,128)(2,1)} %res.1), custom_call_target="tpu_custom_call" | custom-call | flops 8589934592 | bytes 10485760 | tf_op jit(solution)/shard_map/pallas_call | solution.py:394
  113.1 1.7 %copy.7 = bf16[64,2048]{1,0:T(8,128)(2,1)} copy(bf16[64,2048]{1,0:T(8,128)(2,1)} %shard_map.55) | data formatting | bytes 524288

commit v2 on v1

--- a/solution.py
+++ b/solution.py
@@ -15,9 +15,9 @@
 UNITS = 1024
 LANES = 128
 COLS = 2048
-YW = 1280
-ZW = COLS - YW
-YH, ZH = YW // 2, ZW // 2
+Y_CUT = (640, 640)
+Z_CUT = (384, 384)
+YW, ZW = sum(Y_CUT), sum(Z_CUT)
 ROWS = 64
 
 
@@ -61,11 +61,14 @@
 def kernel(
     hid, sgn, w_hbm, expo, res, out,
     slab, recv1, mid, rot, recv2, act, w, w32, part,
-    ys1, yr1, ys2, yr2, zs1, zr1, zs2, zr2, us1, ur1, us2, ur2, vs1, vr1, vs2, vr2,
+    ys1a, ys1b, yr1a, yr1b, ys2, yr2, zs1a, zs1b, zr1a, zr1b, zs2, zr2,
+    us1a, us1b, ur1a, ur1b, us2, ur2, vs1a, vs1b, vr1a, vr1b, vs2, vr2,
     w_sem, a1_sem, a2_send, a2_recv, ag_send, ag_direct, ag_core,
     y_send, yr1_sem, yr2_sem, z_send, zr1_sem, zr2_sem,
     u_send, ur1_sem, ur2_sem, v_send, vr1_sem, vr2_sem,
 ):
+    ys1, yr1, zs1, zr1 = (ys1a, ys1b), (yr1a, yr1b), (zs1a, zs1b), (zr1a, zr1b)
+    us1, ur1, vs1, vr1 = (us1a, us1b), (ur1a, ur1b), (vs1a, vs1b), (vr1a, vr1b)
     m, t = lax.axis_index("mp"), lax.axis_index("tok")
     z, y = lax.div(m, NY), lax.rem(m, NY)
     x, core = lax.div(t, 2), lax.rem(t, 2)
@@ -88,13 +91,15 @@
 
     barrier = pltpu.get_barrier_semaphore()
 
+    def far_first(i):
+        offset = NMP // 2 + lax.div(i + 1, 2) * (1 - 2 * lax.rem(i, 2))
+        return lax.rem(m + offset, NMP)
+
     def greet(i, _):
-        pl.semaphore_signal(
-            barrier, inc=1, device_id=(lax.rem(m + i, NMP), t), device_id_type=MESH
-        )
-        return 0
-
-    lax.fori_loop(1, NMP, greet, 0)
+        pl.semaphore_signal(barrier, inc=1, device_id=(far_first(i), t), device_id_type=MESH)
+        return 0
+
+    lax.fori_loop(0, NMP - 1, greet, 0)
     for dx in (1, 2, 3):
         pl.semaphore_signal(
             barrier, inc=1, device_id=at_x(lax.rem(x + dx, NX), core), device_id_type=MESH
@@ -124,11 +129,11 @@
     pl.semaphore_wait(barrier, NMP - 1 + 4)
 
     def spread(i, _):
-        dest = lax.rem(m + i, NMP)
+        dest = far_first(i)
         send(slab.at[dest], recv1.at[m], a1_sem.at[0], a1_sem.at[1], (dest, t))
         return 0
 
-    lax.fori_loop(1, NMP, spread, 0)
+    lax.fori_loop(0, NMP - 1, spread, 0)
     recv1[m] = slab[m]
 
     def convert(j, _):
@@ -167,15 +172,15 @@
         def one(i, _):
             to_z = lax.rem(z + i, NZ)
             dest = to_z * NY + to_y
-            send(rot.at[dest], recv2.at[j, z], a2_send, a2_recv.at[j], (dest, t))
+            send(rot.at[dest], recv2.at[j, z], a2_send.at[j], a2_recv.at[j], (dest, t))
             return 0
 
         lax.fori_loop(first, NZ, one, 0)
 
+    def given(j):
+        drain(rot.at[pl.ds(0, NZ if j < 3 else NZ - 1)], a2_send.at[j])
+
     give_back(0, ymod(y + 2), 0)
-    give_back(1, ymod(y - 1), 0)
-    give_back(2, ymod(y + 1), 0)
-    give_back(3, y, 1)
     recv2[3, z] = rot[m]
 
     def gather_own(j):
@@ -195,66 +200,70 @@
 
         lax.fori_loop(0, 4, one, 0)
         mine = act.at[j, t]
-        for i, dx in enumerate((1, 3, 2)):
+        for i in (1, 2, 3):
+            dx = x_step(i)
             send(mine, mine, ag_send.at[j], ag_direct.at[j, i], at_x(lax.rem(x + dx, NX), core))
-        send(mine, mine, ag_send.at[j], ag_core.at[j], sibling)
-
-    def pass_on(j):
-        for i, dx in enumerate((1, 3, 2)):
-            piece = act.at[j, lax.rem(x - dx + NX, NX) * 2 + core]
-            drain(piece, ag_direct.at[j, i])
-            send(piece, piece, ag_send.at[j], ag_core.at[j], sibling)
-
-    def multiply(j):
-        drain(act.at[j, pl.ds(0, 4)], ag_core.at[j])
-
-        def one(i, _):
-            cols = pl.ds(pl.multiple_of(i * 256, 256), 256)
-            part[j, :, :, cols] = jnp.dot(
-                act[j].reshape(NZ * ROWS, UNITS), w[:, cols], preferred_element_type=F32
-            ).reshape(NZ, ROWS, 256)
-            return 0
-
-        lax.fori_loop(0, COLS // 256, one, 0)
-
-    def compose(d, step, j, zz, low, half, incoming, dst):
-        this, other = d * half, (1 - d) * half
+        send(mine, mine, ag_send.at[j], ag_core.at[j, 0], sibling)
+
+    def x_step(i):
+        return (0, 1, 3, 2)[i] if isinstance(i, int) else lax.rem(2 * i + 1, 3) + 1
+
+    def chip_from(i):
+        return lax.rem(x - x_step(i) + NX, NX)
+
+    def pass_on(j, i):
+        piece = act.at[j, chip_from(i) * 2 + core]
+        drain(piece, ag_direct.at[j, i])
+        send(piece, piece, ag_send.at[j], ag_core.at[j, i], sibling)
+
+    def multiply(j, i, chip):
+        drain(act.at[j, 0], ag_core.at[j, i])
+        both = pl.ds(chip * 2, 2)
+        part[j, both] = jnp.dot(
+            act[j, both].reshape(2 * ROWS, UNITS), w[...], preferred_element_type=F32
+        ).reshape(2, ROWS, COLS)
+
+    def compose(d, step, j, zz, low, cut, incoming, dst):
+        this, other = d * cut[0], (1 - d) * cut[0]
         if step == 1:
-            dst[...] = part[j, zz, :, pl.ds(low + this, half)].astype(BF16)
+            dst[...] = part[j, zz, :, pl.ds(low + this, cut[d])].astype(BF16)
         elif step == 2:
-            dst[:, pl.ds(this, half)] = (
-                part[j, zz, :, pl.ds(low + this, half)] + incoming[...].astype(F32)
+            dst[:, pl.ds(this, cut[d])] = (
+                part[j, zz, :, pl.ds(low + this, cut[d])] + incoming[...].astype(F32)
             ).astype(BF16)
-            dst[:, pl.ds(other, half)] = part[j, zz, :, pl.ds(low + other, half)].astype(BF16)
+            dst[:, pl.ds(other, cut[1 - d])] = (
+                part[j, zz, :, pl.ds(low + other, cut[1 - d])].astype(BF16)
+            )
         else:
             dst[...] = (
-                part[j, zz, :, pl.ds(low, 2 * half)] + incoming[...].astype(F32)
+                part[j, zz, :, pl.ds(low, sum(cut))] + incoming[...].astype(F32)
             ).astype(BF16)
 
     def z_target(d, step):
         return zmod(z + (5 - step) * (1 - 2 * d))
 
-    def z_hop(j, step, low, half, s1, r1, s2, r2, s_sem, r1_sem, r2_sem):
+    def z_hop(j, step, low, cut, s1, r1, s2, r2, s_sem, r1_sem, r2_sem):
         for d in range(2):
             zz = z_target(d, step)
             if step == 1:
-                compose(d, 1, j, zz, low, half, None, s1.at[d])
-                send(s1.at[d], r1.at[d], s_sem.at[0], r1_sem.at[d], z_next[d])
+                compose(d, 1, j, zz, low, cut, None, s1[d])
+                send(s1[d], r1[d], s_sem.at[d], r1_sem.at[d], z_next[d])
                 continue
             if step == 2:
-                incoming, sem = r1.at[d], r1_sem.at[d]
+                incoming, sem = r1[d], r1_sem.at[d]
             else:
                 incoming, sem = r2.at[d, step - 3], r2_sem.at[d, step - 3]
             drain(incoming, sem)
-            compose(d, step, j, zz, low, half, incoming, s2.at[d, step - 2])
+            compose(d, step, j, zz, low, cut, incoming, s2.at[d, step - 2])
             send(
                 s2.at[d, step - 2], r2.at[d, step - 2],
-                s_sem.at[1], r2_sem.at[d, step - 2], z_next[d],
+                s_sem.at[2], r2_sem.at[d, step - 2], z_next[d],
             )
 
     def z_first(j, step):
         z_hop(
-            j, step, YW, ZH, zs1.at[j], zr1.at[j], zs2.at[j], zr2.at[j],
+            j, step, YW, Z_CUT, [b.at[j] for b in zs1], [b.at[j] for b in zr1],
+            zs2.at[j], zr2.at[j],
             z_send, zr1_sem.at[j], zr2_sem.at[j],
         )
 
@@ -266,96 +275,134 @@
         )
 
     def z_second(step):
-        z_hop(3, step, 0, YH, us1, ur1, us2, ur2, u_send, ur1_sem, ur2_sem)
+        z_hop(3, step, 0, Y_CUT, us1, ur1, us2, ur2, u_send, ur1_sem, ur2_sem)
 
     def block_at(k):
         up = lax.div(k + 1, 2)
         return zmod(z + 4 + up * (1 - 2 * lax.rem(k + 1, 2)))
 
-    def y_first_start(k, _):
+    def y_first_start(chip):
+        for one in range(2):
+            zz = chip * 2 + one
+            for d in range(2):
+                compose(d, 1, 0, zz, 0, Y_CUT, None, ys1[d].at[zz])
+                send(ys1[d].at[zz], yr1[d].at[zz], y_send.at[d], yr1_sem.at[d, zz], y_next[d])
+
+    def y_first_pass(zz):
+        for d in range(2):
+            drain(yr1[d].at[zz], yr1_sem.at[d, zz])
+            compose(d, 2, 1 + d, zz, 0, Y_CUT, yr1[d].at[zz], ys2.at[d, zz])
+            send(ys2.at[d, zz], yr2.at[d, zz], y_send.at[2], yr2_sem.at[d, zz], y_next[d])
+
+    def y_first_other(k, _):
         zz = block_at(k)
-        for d in range(2):
-            compose(d, 1, 0, zz, 0, YH, None, ys1.at[d, k])
-            send(ys1.at[d, k], yr1.at[d, k], y_send.at[0], yr1_sem.at[d, k], y_next[d])
-        return 0
-
-    def y_first_pass(d):
-        def one(k, _):
-            zz = block_at(k)
-            drain(yr1.at[d, k], yr1_sem.at[d, k])
-            compose(d, 2, 1 + d, zz, 0, YH, yr1.at[d, k], ys2.at[d, k])
-            send(ys2.at[d, k], yr2.at[d, k], y_send.at[1], yr2_sem.at[d, k], y_next[d])
-            return 0
-
-        return one
-
-    def y_first_both(k, _):
-        y_first_pass(0)(k, 0)
-        y_first_pass(1)(k, 0)
+
+        @pl.when(lax.div(zz, 2) != x)
+        def _():
+            y_first_pass(zz)
+
         return 0
 
     def y_first_end(k, _):
         zz = block_at(k)
         for d in range(2):
-            drain(yr2.at[d, k], yr2_sem.at[d, k])
+            drain(yr2.at[d, zz], yr2_sem.at[d, zz])
         part[3, zz, :, pl.ds(0, YW)] = (
-            part[3, zz, :, pl.ds(0, YW)] + yr2[0, k].astype(F32) + yr2[1, k].astype(F32)
+            part[3, zz, :, pl.ds(0, YW)] + yr2[0, zz].astype(F32) + yr2[1, zz].astype(F32)
         )
         return 0
 
     def y_second_start():
         for d in range(2):
-            compose(d, 1, 0, z, YW, ZH, None, vs1.at[d])
-            send(vs1.at[d], vr1.at[d], v_send.at[0], vr1_sem.at[d], y_next[d])
+            compose(d, 1, 0, z, YW, Z_CUT, None, vs1[d])
+            send(vs1[d], vr1[d], v_send.at[d], vr1_sem.at[d], y_next[d])
 
     def y_second_pass(d):
-        drain(vr1.at[d], vr1_sem.at[d])
-        compose(d, 2, 1 + d, z, YW, ZH, vr1.at[d], vs2.at[d])
-        send(vs2.at[d], vr2.at[d], v_send.at[1], vr2_sem.at[d], y_next[d])
-
+        drain(vr1[d], vr1_sem.at[d])
+        compose(d, 2, 1 + d, z, YW, Z_CUT, vr1[d], vs2.at[d])
+        send(vs2.at[d], vr2.at[d], v_send.at[2], vr2_sem.at[d], y_next[d])
+
+    def own_chip(j, _):
+        multiply(j, 0, x)
+        return 0
+
+    def first_part(i, _):
+        multiply(0, i, chip_from(i))
+        y_first_start(chip_from(i))
+
+        @pl.when(i == 1)
+        def _():
+            pass_on(0, 3)
+
+        return 0
+
+    def later_part(j):
+        def one(i, _):
+            multiply(j, i, chip_from(i))
+            return 0
+
+        return one
+
+    given(0)
+    give_back(1, ymod(y - 1), 0)
     gather_own(0)
+    given(1)
+    give_back(2, ymod(y + 1), 0)
+    own_chip(0, 0)
+    y_first_start(x)
     gather_own(1)
-    pass_on(0)
+    given(2)
+    give_back(3, y, 1)
+    own_chip(1, 0)
+    pass_on(0, 1)
+    pass_on(0, 2)
     gather_own(2)
+    own_chip(2, 0)
+    lax.fori_loop(1, 4, first_part, 0)
+    z_first(0, 1)
     gather_own(3)
-    multiply(0)
-    z_first(0, 1)
-    lax.fori_loop(0, 8, y_first_start, 0)
-    pass_on(1)
-    multiply(1)
+    y_first_pass(2 * x)
+    pass_on(1, 1)
+    pass_on(1, 2)
+    y_first_pass(2 * x + 1)
+    z_first(0, 2)
+    pass_on(1, 3)
+    own_chip(3, 0)
+    lax.fori_loop(1, 4, later_part(1), 0)
     z_first(1, 1)
-    z_first(0, 2)
-    lax.fori_loop(0, 2, y_first_pass(0), 0)
-    pass_on(2)
-    multiply(2)
+    z_first(0, 3)
+    pass_on(2, 1)
+    pass_on(2, 2)
+    z_first(1, 2)
+    z_first(0, 4)
+    pass_on(2, 3)
+    lax.fori_loop(1, 4, later_part(2), 0)
     z_first(2, 1)
-    z_first(1, 2)
-    z_first(0, 3)
-    lax.fori_loop(0, 2, y_first_pass(1), 0)
-    lax.fori_loop(2, 4, y_first_both, 0)
-    pass_on(3)
-    multiply(3)
+    z_first(1, 3)
+    lax.fori_loop(0, 4, y_first_other, 0)
+    pass_on(3, 1)
+    pass_on(3, 2)
+    z_first(2, 2)
+    z_first(1, 4)
+    pass_on(3, 3)
+    lax.fori_loop(1, 4, later_part(3), 0)
     z_first(3, 1)
-    z_first(2, 2)
-    z_first(1, 3)
-    z_first(0, 4)
-    lax.fori_loop(4, 8, y_first_both, 0)
-    z_first(3, 2)
-    z_first(2, 3)
-    z_first(1, 4)
     z_first_end(0)
     y_second_start()
+    z_first(2, 3)
+    lax.fori_loop(4, 8, y_first_other, 0)
+    z_first(3, 2)
+    z_first_end(1)
+    z_first(2, 4)
     lax.fori_loop(0, 1, y_first_end, 0)
     z_second(1)
+    y_second_pass(0)
     z_first(3, 3)
-    z_first(2, 4)
-    z_first_end(1)
-    y_second_pass(0)
+    z_first_end(2)
+    y_second_pass(1)
     lax.fori_loop(1, 3, y_first_end, 0)
     z_second(2)
     z_first(3, 4)
-    z_first_end(2)
-    y_second_pass(1)
     lax.fori_loop(3, 5, y_first_end, 0)
     z_second(3)
     z_first_end(3)
@@ -374,14 +421,14 @@
     out[:, :YW] = (res[:, :YW].astype(F32) + total * scales[:, :YW]).astype(BF16)
 
     drain(slab.at[pl.ds(0, NMP - 1)], a1_sem.at[0])
-    drain(rot.at[pl.ds(0, NMP - 1)], a2_send)
+    given(3)
     for j in range(4):
         drain(act.at[j, pl.ds(0, 7)], ag_send.at[j])
-    for buf, sem in (
-        (ys1, y_send.at[0]), (ys2, y_send.at[1]), (zs1, z_send.at[0]), (zs2, z_send.at[1]),
-        (us1, u_send.at[0]), (us2, u_send.at[1]), (vs1, v_send.at[0]), (vs2, v_send.at[1]),
+    for first, second, sems in (
+        (ys1, ys2, y_send), (zs1, zs2, z_send), (us1, us2, u_send), (vs1, vs2, v_send),
     ):
-        drain(buf, sem)
+        for buf, sem in ((first[0], sems.at[0]), (first[1], sems.at[1]), (second, sems.at[2])):
+            drain(buf, sem)
 
 
 def per_device(hidden, sign_bits, down_weight, exponents, residual):
@@ -389,6 +436,9 @@
 
     def pair(*shape):
         return [pltpu.VMEM(shape, BF16)] * 2
+
+    def split(shape, cut):
+        return [pltpu.VMEM(shape + (width,), BF16) for width in cut] * 2
 
     dma = pltpu.SemaphoreType.DMA
     return pl.pallas_call(
@@ -406,17 +456,13 @@
             pltpu.VMEM((UNITS, COLS), BF16),
             pltpu.VMEM((UNITS, COLS), jnp.int32),
             pltpu.VMEM((4, NZ, ROWS, COLS), F32),
-            *pair(2, 8, ROWS, YH),
-            *pair(2, 8, ROWS, YW),
-            *pair(4, 2, ROWS, ZH),
-            *pair(4, 2, 3, ROWS, ZW),
-            *pair(2, ROWS, YH),
-            *pair(2, 3, ROWS, YW),
-            *pair(2, ROWS, ZH),
-            *pair(2, ROWS, ZW),
-            dma((8,)), dma((2,)), dma, dma((4,)), dma((4,)), dma((4, 3)), dma((4,)),
-            dma((2,)), dma((2, 8)), dma((2, 8)), dma((2,)), dma((4, 2)), dma((4, 2, 3)),
-            dma((2,)), dma((2,)), dma((2, 3)), dma((2,)), dma((2,)), dma((2,)),
+            *split((8, ROWS), Y_CUT), *pair(2, 8, ROWS, YW),
+            *split((4, ROWS), Z_CUT), *pair(4, 2, 3, ROWS, ZW),
+            *split((ROWS,), Y_CUT), *pair(2, 3, ROWS, YW),
+            *split((ROWS,), Z_CUT), *pair(2, ROWS, ZW),
+            dma((8,)), dma((2,)), dma((4,)), dma((4,)), dma((4,)), dma((4, 4)), dma((4, 4)),
+            dma((3,)), dma((2, 8)), dma((2, 8)), dma((3,)), dma((4, 2)), dma((4, 2, 3)),
+            dma((3,)), dma((2,)), dma((2, 3)), dma((3,)), dma((2,)), dma((2,)),
         ],
         compiler_params=pltpu.CompilerParams(
             collective_id=0, has_side_effects=True, vmem_limit_bytes=60 * 2**20

time: 116 us -> 100 us (0.86); the launches traced: 115 us -> 100 us
  Pallas kernels: 113 us -> 98.4 us
    pallas_call x1, Pallas kernels: 113 us -> 98.4 us  [per_device(): pl.pallas_call(kernel, out_shape=jax.ShapeDtypeStruct((ROWS, COLS), BF16)...]
where the time goes in v2:
time: 100 us
  Pallas kernels  98.4 us (98%)
  local copies, waits for them, and re-layouts  1.67 us (2%)
    pallas_call x1, Pallas kernels, per_device(): pl.pallas_call(kernel, out_shape=jax.ShapeDtypeStruct((ROWS, COLS), BF16)...  98.4 us

profile of v2, /device:TPU:2, one launch (start us, length us, event | category | flops | bytes accessed | tf_op | source)
XLA Modules:
  0.0 100.0 jit_solution(325719996028180134)
XLA Ops:
  0.0 98.4 %shard_map.55 = bf16[64,2048]{1,0:T(8,128)(2,1)} custom-call(bf16[256,1024]{1,0:T(8,128)(2,1)} %hid.1, s32[1,1024]{1,0:T(1,128)} %bitcast.3, s32[1024,2048]{1,0:T(8,128)} %w_hbm.1, s32[1,2048]{1,0:T(1,128)} %bitcast.2, bf16[64,2048]{1,0:T(8,128)(2,1)} %res.1), custom_call_target="tpu_custom_call" | custom-call | flops 8589934592 | bytes 10485760 | tf_op jit(solution)/shard_map/pallas_call | solution.py:444
  98.4 1.7 %copy.7 = bf16[64,2048]{1,0:T(8,128)(2,1)} copy(bf16[64,2048]{1,0:T(8,128)(2,1)} %shard_map.55) | data formatting | bytes 524288

commit v3 on v2

--- a/solution.py
+++ b/solution.py
@@ -379,7 +379,7 @@
     lax.fori_loop(1, 4, later_part(2), 0)
     z_first(2, 1)
     z_first(1, 3)
-    lax.fori_loop(0, 4, y_first_other, 0)
+    lax.fori_loop(0, 2, y_first_other, 0)
     pass_on(3, 1)
     pass_on(3, 2)
     z_first(2, 2)
@@ -387,27 +387,30 @@
     pass_on(3, 3)
     lax.fori_loop(1, 4, later_part(3), 0)
     z_first(3, 1)
+    z_first(2, 3)
     z_first_end(0)
+    lax.fori_loop(2, 4, y_first_other, 0)
     y_second_start()
-    z_first(2, 3)
-    lax.fori_loop(4, 8, y_first_other, 0)
     z_first(3, 2)
+    z_first(2, 4)
     z_first_end(1)
-    z_first(2, 4)
     lax.fori_loop(0, 1, y_first_end, 0)
     z_second(1)
-    y_second_pass(0)
+    lax.fori_loop(4, 5, y_first_other, 0)
     z_first(3, 3)
     z_first_end(2)
-    y_second_pass(1)
     lax.fori_loop(1, 3, y_first_end, 0)
     z_second(2)
+    lax.fori_loop(5, 7, y_first_other, 0)
     z_first(3, 4)
     lax.fori_loop(3, 5, y_first_end, 0)
     z_second(3)
-    z_first_end(3)
+    lax.fori_loop(7, 8, y_first_other, 0)
+    y_second_pass(0)
+    y_second_pass(1)
     lax.fori_loop(5, 7, y_first_end, 0)
     z_second(4)
+    z_first_end(3)
     lax.fori_loop(7, 8, y_first_end, 0)
 
     scales = jnp.exp2(-expo[...].astype(F32))

time: 100 us -> 100 us (level)
  no operation moved by 1% of the time
where the time goes in v3:
time: 100 us
  Pallas kernels  98.4 us (98%)
  local copies, waits for them, and re-layouts  1.67 us (2%)
    pallas_call x1, Pallas kernels, per_device(): pl.pallas_call(kernel, out_shape=jax.ShapeDtypeStruct((ROWS, COLS), BF16)...  98.4 us

profile of v3, /device:TPU:2, one launch (start us, length us, event | category | flops | bytes accessed | tf_op | source)
XLA Modules:
  0.0 100.0 jit_solution(1077318521655472942)
XLA Ops:
  0.0 98.4 %shard_map.55 = bf16[64,2048]{1,0:T(8,128)(2,1)} custom-call(bf16[256,1024]{1,0:T(8,128)(2,1)} %hid.1, s32[1,1024]{1,0:T(1,128)} %bitcast.3, s32[1024,2048]{1,0:T(8,128)} %w_hbm.1, s32[1,2048]{1,0:T(1,128)} %bitcast.2, bf16[64,2048]{1,0:T(8,128)(2,1)} %res.1), custom_call_target="tpu_custom_call" | custom-call | flops 8589934592 | bytes 10485760 | tf_op jit(solution)/shard_map/pallas_call | solution.py:447
  98.4 1.7 %copy.7 = bf16[64,2048]{1,0:T(8,128)(2,1)} copy(bf16[64,2048]{1,0:T(8,128)(2,1)} %shard_map.55) | data formatting | bytes 524288

commit v4 on v3

--- a/solution.py
+++ b/solution.py
@@ -63,7 +63,7 @@
     slab, recv1, mid, rot, recv2, act, w, w32, part,
     ys1a, ys1b, yr1a, yr1b, ys2, yr2, zs1a, zs1b, zr1a, zr1b, zs2, zr2,
     us1a, us1b, ur1a, ur1b, us2, ur2, vs1a, vs1b, vr1a, vr1b, vs2, vr2,
-    w_sem, a1_sem, a2_send, a2_recv, ag_send, ag_direct, ag_core,
+    w_sem, a1_sem, a2_send, a2_recv, ag_send, ag_direct, ag_far, ag_core,
     y_send, yr1_sem, yr2_sem, z_send, zr1_sem, zr2_sem,
     u_send, ur1_sem, ur2_sem, v_send, vr1_sem, vr2_sem,
 ):
@@ -87,6 +87,7 @@
 
     sibling = at_x(x, 1 - core)
     y_next = (at_zy(z, ymod(y + 1)), at_zy(z, ymod(y - 1)))
+    x_next = (at_x(lax.rem(x + 1, NX), core), at_x(lax.rem(x + 3, NX), core))
     z_next = (at_zy(zmod(z + 1), y), at_zy(zmod(z - 1), y))
 
     barrier = pltpu.get_barrier_semaphore()
@@ -200,9 +201,8 @@
 
         lax.fori_loop(0, 4, one, 0)
         mine = act.at[j, t]
-        for i in (1, 2, 3):
-            dx = x_step(i)
-            send(mine, mine, ag_send.at[j], ag_direct.at[j, i], at_x(lax.rem(x + dx, NX), core))
+        for i in (1, 2):
+            send(mine, mine, ag_send.at[j], ag_direct.at[j, i], x_next[i - 1])
         send(mine, mine, ag_send.at[j], ag_core.at[j, 0], sibling)
 
     def x_step(i):
@@ -212,8 +212,16 @@
         return lax.rem(x - x_step(i) + NX, NX)
 
     def pass_on(j, i):
-        piece = act.at[j, chip_from(i) * 2 + core]
-        drain(piece, ag_direct.at[j, i])
+        source = chip_from(i) * 2 + core
+        piece = act.at[j, source]
+        halves = [act.at[j, source, pl.ds(0, ROWS // 2)], act.at[j, source, pl.ds(ROWS // 2, ROWS // 2)]]
+        if i < 3:
+            drain(piece, ag_direct.at[j, i])
+            half = halves[i - 1]
+            send(half, half, ag_send.at[j], ag_far.at[j, i - 1], x_next[i - 1])
+        else:
+            for one in range(2):
+                drain(halves[one], ag_far.at[j, one])
         send(piece, piece, ag_send.at[j], ag_core.at[j, i], sibling)
 
     def multiply(j, i, chip):
@@ -463,7 +471,7 @@
             *split((4, ROWS), Z_CUT), *pair(4, 2, 3, ROWS, ZW),
             *split((ROWS,), Y_CUT), *pair(2, 3, ROWS, YW),
             *split((ROWS,), Z_CUT), *pair(2, ROWS, ZW),
-            dma((8,)), dma((2,)), dma((4,)), dma((4,)), dma((4,)), dma((4, 4)), dma((4, 4)),
+            dma((8,)), dma((2,)), dma((4,)), dma((4,)), dma((4,)), dma((4, 4)), dma((4, 2)), dma((4, 4)),
             dma((3,)), dma((2, 8)), dma((2, 8)), dma((3,)), dma((4, 2)), dma((4, 2, 3)),
             dma((3,)), dma((2,)), dma((2, 3)), dma((3,)), dma((2,)), dma((2,)),
         ],

time: 100 us -> 104 us (1.040)
  Pallas kernels: 98.4 us -> 102 us
    pallas_call x1, Pallas kernels: 98.4 us -> 102 us  [per_device(): pl.pallas_call(kernel, out_shape=jax.ShapeDtypeStruct((ROWS, COLS), BF16)...]
where the time goes in v4:
time: 104 us
  Pallas kernels  102 us (98%)
  local copies, waits for them, and re-layouts  1.67 us (2%)
    pallas_call x1, Pallas kernels, per_device(): pl.pallas_call(kernel, out_shape=jax.ShapeDtypeStruct((ROWS, COLS), BF16)...  102 us

profile of v4, /device:TPU:2, one launch (start us, length us, event | category | flops | bytes accessed | tf_op | source)
XLA Modules:
  0.0 103.8 jit_solution(707601956452579246)
XLA Ops:
  0.0 102.1 %shard_map.55 = bf16[64,2048]{1,0:T(8,128)(2,1)} custom-call(bf16[256,1024]{1,0:T(8,128)(2,1)} %hid.1, s32[1,1024]{1,0:T(1,128)} %bitcast.3, s32[1024,2048]{1,0:T(8,128)} %w_hbm.1, s32[1,2048]{1,0:T(1,128)} %bitcast.2, bf16[64,2048]{1,0:T(8,128)(2,1)} %res.1), custom_call_target="tpu_custom_call" | custom-call | flops 8589934592 | bytes 10485760 | tf_op jit(solution)/shard_map/pallas_call | solution.py:455
  102.1 1.7 %copy.7 = bf16[64,2048]{1,0:T(8,128)(2,1)} copy(bf16[64,2048]{1,0:T(8,128)(2,1)} %shard_map.55) | data formatting | bytes 524288

commit v5 on v3

--- a/solution.py
+++ b/solution.py
@@ -63,7 +63,7 @@
     slab, recv1, mid, rot, recv2, act, w, w32, part,
     ys1a, ys1b, yr1a, yr1b, ys2, yr2, zs1a, zs1b, zr1a, zr1b, zs2, zr2,
     us1a, us1b, ur1a, ur1b, us2, ur2, vs1a, vs1b, vr1a, vr1b, vs2, vr2,
-    w_sem, a1_sem, a2_send, a2_recv, ag_send, ag_direct, ag_core,
+    ring_sem, w_sem, a1_sem, a2_send, a2_recv, ag_send, ag_direct, ag_core,
     y_send, yr1_sem, yr2_sem, z_send, zr1_sem, zr2_sem,
     u_send, ur1_sem, ur2_sem, v_send, vr1_sem, vr2_sem,
 ):
@@ -95,11 +95,13 @@
         offset = NMP // 2 + lax.div(i + 1, 2) * (1 - 2 * lax.rem(i, 2))
         return lax.rem(m + offset, NMP)
 
-    def greet(i, _):
-        pl.semaphore_signal(barrier, inc=1, device_id=(far_first(i), t), device_id_type=MESH)
-        return 0
-
-    lax.fori_loop(0, NMP - 1, greet, 0)
+    def greet(device):
+        pl.semaphore_signal(barrier, inc=1, device_id=device, device_id_type=MESH)
+
+    for dz in (4, 3, 5, 2, 6, 1, 7):
+        greet(at_zy(zmod(z + dz), y))
+    for dy in (2, 1, 3):
+        greet(at_zy(z, ymod(y + dy)))
     for dx in (1, 2, 3):
         pl.semaphore_signal(
             barrier, inc=1, device_id=at_x(lax.rem(x + dx, NX), core), device_id_type=MESH
@@ -126,7 +128,12 @@
         return 0
 
     lax.fori_loop(0, 16, build, 0)
-    pl.semaphore_wait(barrier, NMP - 1 + 4)
+    pl.semaphore_wait(barrier, NZ - 1 + NY - 1 + 4)
+    for dy in (2, 1, 3):
+        pl.semaphore_signal(
+            ring_sem, inc=1, device_id=at_zy(z, ymod(y + dy)), device_id_type=MESH
+        )
+    pl.semaphore_wait(ring_sem, NY - 1)
 
     def spread(i, _):
         dest = far_first(i)
@@ -463,6 +470,7 @@
             *split((4, ROWS), Z_CUT), *pair(4, 2, 3, ROWS, ZW),
             *split((ROWS,), Y_CUT), *pair(2, 3, ROWS, YW),
             *split((ROWS,), Z_CUT), *pair(2, ROWS, ZW),
+            pltpu.SemaphoreType.REGULAR,
             dma((8,)), dma((2,)), dma((4,)), dma((4,)), dma((4,)), dma((4, 4)), dma((4, 4)),
             dma((3,)), dma((2, 8)), dma((2, 8)), dma((3,)), dma((4, 2)), dma((4, 2, 3)),
             dma((3,)), dma((2,)), dma((2, 3)), dma((3,)), dma((2,)), dma((2,)),

time: 100 us -> 101 us (1.010)
  no operation moved by 1% of the time
where the time goes in v5:
time: 101 us; the launch traced here: 100 us
  Pallas kernels  98.5 us (98%)
  local copies, waits for them, and re-layouts  1.67 us (2%)
    pallas_call x1, Pallas kernels, per_device(): pl.pallas_call(kernel, out_shape=jax.ShapeDtypeStruct((ROWS, COLS), BF16)...  98.5 us

profile of v5, /device:TPU:2, one launch (start us, length us, event | category | flops | bytes accessed | tf_op | source)
XLA Modules:
  0.0 100.2 jit_solution(16214796168942929097)
XLA Ops:
  0.0 98.5 %shard_map.55 = bf16[64,2048]{1,0:T(8,128)(2,1)} custom-call(bf16[256,1024]{1,0:T(8,128)(2,1)} %hid.1, s32[1,1024]{1,0:T(1,128)} %bitcast.3, s32[1024,2048]{1,0:T(8,128)} %w_hbm.1, s32[1,2048]{1,0:T(1,128)} %bitcast.2, bf16[64,2048]{1,0:T(8,128)(2,1)} %res.1), custom_call_target="tpu_custom_call" | custom-call | flops 8589934592 | bytes 10485760 | tf_op jit(solution)/shard_map/pallas_call | solution.py:454
  98.5 1.7 %copy.7 = bf16[64,2048]{1,0:T(8,128)(2,1)} copy(bf16[64,2048]{1,0:T(8,128)(2,1)} %shard_map.55) | data formatting | bytes 524288
